TPU v7x, 128 devices: a whole 4x4x4 slice. The times are simulated.
128 devices in a mesh: seq: 8 (over y, core), chan: 16 (over x, z).
Axes of the slice: x: 4, y: 4, z: 4, core: 2. Of those that a mesh axis runs over, the one named last changes fastest.
Arguments:
- query_proj: bfloat16 [16384, 4096], P(('seq', 'chan')), may hold values from -6 to 6
- key_proj: bfloat16 [16384, 4096], P(('seq', 'chan')), may hold values from -6 to 6
- value_proj: bfloat16 [16384, 4096], P(('seq', 'chan')), may hold values from -6 to 6
- filter_taps: bfloat16 [16384, 4096], P(('seq', 'chan')), may hold values from -0.046875 to 0.046875
- skip_gain: float32 [4096], replicated, may hold values from 0.5 to 1.5
Outputs:
- mixed: bfloat16 [16384, 4096], P(('seq', 'chan'))
All inputs are finite; a program needn't handle non-finite values.
Results may differ from a plain program's by a relative error of at most 0.012.
Values may be sent and summed in bfloat16 or wider, within the bound.
A program may use at most 256 MiB of HBM per device.

v0:
```python
import functools
import math

import jax
import jax.numpy as jnp
import numpy as np
from jax import lax
from jax.experimental import pallas as pl
from jax.experimental.pallas import tpu as pltpu
from jax.sharding import PartitionSpec as P

MESH = pl.DeviceIdType.MESH
DEVS = 128
TOK = 128
CHUNKS = 2
CC = 16
BLOCKS = 16
F32 = jnp.float32
BF16 = jnp.bfloat16


def tables():
    idx = np.arange(128)
    coarse = 2.0 * math.pi * np.outer(idx + 0.5, idx) / 256.0
    twist = 2.0 * math.pi * np.outer(idx + 0.5, idx) / 32768.0
    inner = 2.0 * math.pi * (np.outer(idx, idx) % 128) / 128.0
    fwd_outer = np.concatenate([np.cos(coarse), -np.sin(coarse)], axis=0)
    cos_in, sin_in = np.cos(inner), np.sin(inner)
    fwd_inner = np.block([[cos_in, -sin_in], [sin_in, cos_in]])
    inv_inner = np.block([[cos_in, sin_in], [-sin_in, cos_in]])
    inv_outer = np.concatenate([np.cos(coarse.T), -np.sin(coarse.T)], axis=1) * (2.0 / 32768.0)
    twists = np.stack([np.cos(twist), -np.sin(twist)])
    return (
        fwd_outer.astype(jnp.bfloat16),
        fwd_inner.astype(jnp.bfloat16),
        inv_inner.astype(jnp.bfloat16),
        inv_outer.astype(jnp.bfloat16),
        twists.astype(np.float32),
    )


def group_device(group):
    x = (group // 64) * 2 + (group // 4) % 2
    y = ((group // 32) % 2) * 2 + (group // 2) % 2
    z = ((group // 16) % 2) * 2 + group % 2
    core = (group // 8) % 2
    return y * 2 + core, x * 4 + z


def own_group(seq, chan):
    x, z = chan // 4, chan % 4
    y, core = seq // 2, seq % 2
    return (x // 2) * 64 + (y // 2) * 32 + (z // 2) * 16 + core * 8 + (x % 2) * 4 + (y % 2) * 2 + z % 2


def kernel(
    q_hbm, k_hbm, v_hbm, h_hbm, gain_hbm, fo_hbm, fi_hbm, ii_hbm, io_hbm, tw_hbm, out_hbm,
    q_buf, k_buf, v_buf, h_buf, gain_buf, fo_buf, fi_buf, ii_buf, io_buf, tw_buf, out_buf,
    send, recv, wide, ywide, ysend, yrecv,
    in_sem, out_sem, send_sem, recv_sem, own_sem, ysend_sem, yrecv_sem, yown_sem,
):
    seq, chan = lax.axis_index("seq"), lax.axis_index("chan")
    me = seq * 16 + chan
    group_me = own_group(seq, chan)

    pairs = (
        (k_hbm, k_buf), (v_hbm, v_buf), (h_hbm, h_buf), (fo_hbm, fo_buf), (fi_hbm, fi_buf), (ii_hbm, ii_buf),
        (io_hbm, io_buf), (tw_hbm, tw_buf), (q_hbm, q_buf), (gain_hbm, gain_buf),
    )
    loads = [pltpu.make_async_copy(src, dst, in_sem.at[i]) for i, (src, dst) in enumerate(pairs)]
    for load in loads:
        load.start()

    barrier = pltpu.get_barrier_semaphore()

    def greet(step, carry):
        peer = (me + step) % DEVS
        pl.semaphore_signal(barrier, inc=1, device_id=(peer // 16, peer % 16), device_id_type=MESH)
        return carry

    lax.fori_loop(1, DEVS, greet, 0)
    for load in loads[:3]:
        load.wait()
    pl.semaphore_wait(barrier, DEVS - 1)

    def pack(chunk, step, carry):
        block = (group_me // 8 + step) % BLOCKS
        lanes = pl.ds(pl.multiple_of(chunk * (BLOCKS * 128) + block * 128, 128), 128)
        product = (k_buf[:, lanes].astype(F32) * v_buf[:, lanes].astype(F32)).astype(BF16)
        send[chunk, pl.ds(block * 8, 8), 0] = product.T.reshape(8, CC, TOK)
        send[chunk, pl.ds(block * 8, 8), 1] = h_buf[:, lanes].T.reshape(8, CC, TOK)
        for near in range(8):
            group = block * 8 + (group_me + near) % 8
            seq_to, chan_to = group_device(group)

            @pl.when(group != group_me)
            def _():
                pltpu.make_async_remote_copy(
                    src_ref=send.at[chunk, group], dst_ref=recv.at[chunk, me],
                    send_sem=send_sem.at[chunk], recv_sem=recv_sem.at[chunk],
                    device_id=(seq_to, chan_to), device_id_type=MESH,
                ).start()

            @pl.when(group == group_me)
            def _():
                pltpu.make_async_copy(send.at[chunk, group], recv.at[chunk, me], own_sem.at[chunk]).start()

        return carry

    for chunk in range(CHUNKS):
        lax.fori_loop(0, BLOCKS, functools.partial(pack, chunk), 0)

    for load in loads[3:]:
        load.wait()

    others = pl.ds(0, DEVS - 1)

    def widen(chunk, step, carry):
        part = pl.ds(step * 8, 8)
        rows = pl.ds(pl.multiple_of(step * (8 * 2 * CC), 8 * 2 * CC), 8 * 2 * CC)
        wide[rows, :] = recv[chunk, part].reshape(8 * 2 * CC, TOK).astype(F32)
        return carry

    def transform(at, carry):
        twist_re, twist_im = tw_buf[0], tw_buf[1]
        turned = []
        for c in (2 * at, 2 * at + 1):
            x = wide[pl.ds(c, DEVS, 2 * CC), :].astype(BF16)
            h = wide[pl.ds(CC + c, DEVS, 2 * CC), :].astype(BF16)
            both = jnp.dot(fo_buf[...], jnp.concatenate([x, h], axis=1), preferred_element_type=F32)
            rows = []
            for lane in (0, 128):
                re, im = both[:128, lane:lane + 128], both[128:, lane:lane + 128]
                rows.append(jnp.concatenate(
                    [(re * twist_re - im * twist_im).astype(BF16), (re * twist_im + im * twist_re).astype(BF16)], axis=1))
            spectra = jnp.dot(jnp.concatenate(rows, axis=0), fi_buf[...], preferred_element_type=F32)
            x_re, x_im = spectra[:128, :128], spectra[:128, 128:]
            h_re, h_im = spectra[128:, :128], spectra[128:, 128:]
            mixed = jnp.concatenate(
                [(x_re * h_re - x_im * h_im).astype(BF16), (x_re * h_im + x_im * h_re).astype(BF16)], axis=1)
            back = jnp.dot(mixed, ii_buf[...], preferred_element_type=F32)
            re, im = back[:, :128], back[:, 128:]
            turned.append(jnp.concatenate(
                [(re * twist_re + im * twist_im).astype(BF16), (im * twist_re - re * twist_im).astype(BF16)], axis=0))
        y = jnp.dot(io_buf[...], jnp.concatenate(turned, axis=1), preferred_element_type=F32)
        ywide[pl.ds(2 * at, DEVS, CC), :] = y[:, :128]
        ywide[pl.ds(2 * at + 1, DEVS, CC), :] = y[:, 128:]
        return carry

    def give_back(chunk, step, carry):
        peer = (me + step) % DEVS
        ysend[chunk, peer] = ywide[pl.ds(pl.multiple_of(peer * CC, CC), CC), :].astype(BF16)

        @pl.when(step != 0)
        def _():
            pltpu.make_async_remote_copy(
                src_ref=ysend.at[chunk, peer], dst_ref=yrecv.at[chunk, group_me],
                send_sem=ysend_sem.at[chunk], recv_sem=yrecv_sem.at[chunk],
                device_id=(peer // 16, peer % 16), device_id_type=MESH,
            ).start()

        @pl.when(step == 0)
        def _():
            pltpu.make_async_copy(ysend.at[chunk, peer], yrecv.at[chunk, group_me], yown_sem.at[chunk]).start()

        return carry

    for chunk in range(CHUNKS):
        arrived = recv.at[chunk, others]
        pltpu.make_async_copy(arrived, arrived, recv_sem.at[chunk]).wait()
        pltpu.make_async_copy(recv.at[chunk, 0], recv.at[chunk, 0], own_sem.at[chunk]).wait()
        lax.fori_loop(0, 16, functools.partial(widen, chunk), 0)
        lax.fori_loop(0, CC // 2, transform, 0)
        lax.fori_loop(0, DEVS, functools.partial(give_back, chunk), 0)

    def gate(chunk, block, carry):
        lanes = pl.ds(pl.multiple_of(chunk * (BLOCKS * 128) + block * 128, 128), 128)
        convolved = yrecv[chunk, pl.ds(block * 8, 8)].reshape(128, TOK).T.astype(F32)
        product = (k_buf[:, lanes].astype(F32) * v_buf[:, lanes].astype(F32)).astype(BF16).astype(F32)
        out_buf[:, lanes] = (q_buf[:, lanes].astype(F32) * (convolved + gain_buf[:, lanes] * product)).astype(BF16)
        return carry

    stores = []
    for chunk in range(CHUNKS):
        arrived = yrecv.at[chunk, others]
        pltpu.make_async_copy(arrived, arrived, yrecv_sem.at[chunk]).wait()
        pltpu.make_async_copy(yrecv.at[chunk, 0], yrecv.at[chunk, 0], yown_sem.at[chunk]).wait()
        lax.fori_loop(0, BLOCKS, functools.partial(gate, chunk), 0)
        half = pl.ds(chunk * BLOCKS * 128, BLOCKS * 128)
        stores.append(pltpu.make_async_copy(out_buf.at[:, half], out_hbm.at[:, half], out_sem.at[chunk]))
        stores[-1].start()
    for store in stores:
        store.wait()
    for chunk in range(CHUNKS):
        left = send.at[chunk, others]
        pltpu.make_async_copy(left, left, send_sem.at[chunk]).wait()
        left = ysend.at[chunk, others]
        pltpu.make_async_copy(left, left, ysend_sem.at[chunk]).wait()


def shards(query_proj, key_proj, value_proj, filter_taps, skip_gain):
    whole = (TOK, 4096)
    any_spec = pl.BlockSpec(memory_space=pltpu.HBM)
    return pl.pallas_call(
        kernel,
        out_shape=jax.ShapeDtypeStruct(whole, BF16),
        in_specs=[any_spec] * 10,
        out_specs=any_spec,
        scratch_shapes=[
            pltpu.VMEM(whole, BF16), pltpu.VMEM(whole, BF16), pltpu.VMEM(whole, BF16), pltpu.VMEM(whole, BF16),
            pltpu.VMEM((1, 4096), F32),
            pltpu.VMEM((256, 128), BF16), pltpu.VMEM((256, 256), BF16), pltpu.VMEM((256, 256), BF16),
            pltpu.VMEM((128, 256), BF16), pltpu.VMEM((2, 128, 128), F32),
            pltpu.VMEM(whole, BF16),
            pltpu.VMEM((CHUNKS, DEVS, 2, CC, TOK), BF16), pltpu.VMEM((CHUNKS, DEVS, 2, CC, TOK), BF16),
            pltpu.VMEM((DEVS * 2 * CC, TOK), F32), pltpu.VMEM((DEVS * CC, TOK), F32),
            pltpu.VMEM((CHUNKS, DEVS, CC, TOK), BF16), pltpu.VMEM((CHUNKS, DEVS, CC, TOK), BF16),
            pltpu.SemaphoreType.DMA((10,)), pltpu.SemaphoreType.DMA((CHUNKS,)),
            pltpu.SemaphoreType.DMA((CHUNKS,)), pltpu.SemaphoreType.DMA((CHUNKS,)), pltpu.SemaphoreType.DMA((CHUNKS,)),
            pltpu.SemaphoreType.DMA((CHUNKS,)), pltpu.SemaphoreType.DMA((CHUNKS,)), pltpu.SemaphoreType.DMA((CHUNKS,)),
        ],
        compiler_params=pltpu.CompilerParams(
            collective_id=0, has_side_effects=True, vmem_limit_bytes=60 << 20
        ),
        cost_estimate=pl.CostEstimate(flops=3 << 30, bytes_accessed=6 << 20, transcendentals=0),
        name="long_conv",
    )(query_proj, key_proj, value_proj, filter_taps, skip_gain.reshape(1, 4096), *(jnp.asarray(t) for t in tables()))


def solution(mesh):
    split = P(("seq", "chan"), None)
    return jax.shard_map(
        shards, mesh=mesh, in_specs=(split, split, split, split, P()), out_specs=split, check_vma=False
    )
```

profile of v0, /device:TPU:1, one launch (start us, length us, event | category | flops | bytes accessed | tf_op | source)
XLA Modules:
  0.0 70.4 jit_solution(1824066754809916765)
XLA Ops:
  0.0 68.1 %long_conv.1 = bf16[128,4096]{1,0:T(8,128)(2,1)} custom-call(bf16[128,4096]{1,0:T(8,128)(2,1)} %q_hbm.1, bf16[128,4096]{1,0:T(8,128)(2,1)} %k_hbm.1, bf16[128,4096]{1,0:T(8,128)(2,1)} %v_hbm.1, bf16[128,4096]{1,0:T(8,128)(2,1)} %h_hbm.1, f32[1,4096]{1,0:T(1,128)} %bitcast.1, bf16[256,128]{1,0:T(8,128)(2,1)} %constant.10.clone.fo_hbm, ...), custom_call_target="tpu_custom_call" | custom-call | flops 3221225472 | bytes 6291456 | tf_op jit(solution)/shard_map/long_conv/pallas_call | solution.py:204
  68.1 2.3 %copy.12 = bf16[128,4096]{1,0:T(8,128)(2,1)} copy(bf16[128,4096]{1,0:T(8,128)(2,1)} %long_conv.1) | data formatting | bytes 2097152
where the time goes:
time: 70.8 us; the launch traced here: 70.4 us
  Pallas kernels  68.1 us (96%)
  local copies, waits for them, and re-layouts  2.29 us (3%)
    pallas_call x1, Pallas kernels, shards(): pl.pallas_call(kernel, out_shape=jax.ShapeDtypeStruct(whole, BF16), in_sp...  68.1 us
    unnamed x1, local copies, waits for them, and re-layouts  2.29 us

commit v1 on v0

v1 whole, which is shorter than its diff:
```python
import functools
import math

import jax
import jax.numpy as jnp
import numpy as np
from jax import lax
from jax.experimental import pallas as pl
from jax.experimental.pallas import tpu as pltpu
from jax.sharding import PartitionSpec as P

MESH = pl.DeviceIdType.MESH
DEVS = 128
TOK = 128
CHUNKS = 2
CC = 16
BATCH = 16
UNROLL = 4
BLOCKS = 16
F32 = jnp.float32
BF16 = jnp.bfloat16


def tables():
    idx = np.arange(128)
    coarse = 2.0 * math.pi * np.outer(idx + 0.5, idx) / 256.0
    twist = 2.0 * math.pi * np.outer(idx + 0.5, idx) / 32768.0
    inner = 2.0 * math.pi * (np.outer(idx, idx) % 128) / 128.0
    fwd_outer = np.concatenate([np.cos(coarse), -np.sin(coarse)], axis=0)
    cos_in, sin_in = np.cos(inner), np.sin(inner)
    fwd_inner = np.block([[cos_in, -sin_in], [sin_in, cos_in]])
    inv_inner = np.block([[cos_in, sin_in], [-sin_in, cos_in]])
    inv_outer = np.concatenate([np.cos(coarse.T), -np.sin(coarse.T)], axis=1) * (2.0 / 32768.0)
    twists = np.stack([np.cos(twist), -np.sin(twist)])
    return (
        fwd_outer.astype(jnp.bfloat16),
        fwd_inner.astype(jnp.bfloat16),
        inv_inner.astype(jnp.bfloat16),
        inv_outer.astype(jnp.bfloat16),
        twists.astype(np.float32),
    )


def sweep(visit):
    seq, chan = lax.axis_index("seq"), lax.axis_index("chan")
    here = (chan // 4, seq // 2, chan % 4)
    cores = (seq % 2, 1 - seq % 2)
    fixed = [[lax.rem(at + far, 4) for far in range(4)] for at in here]

    def go(place, core):
        seq_to, chan_to = place[1] * 2 + cores[core], place[0] * 4 + place[2]
        visit(seq_to * 16 + chan_to, (seq_to, chan_to))

    def moving(turn):
        fars = (turn + 1, lax.rem(turn + 1, 3) + 1, lax.rem(turn + 2, 3) + 1)
        return [[lax.rem(at + far, 4) for far in fars] for at in here]

    def three_axes(turn, carry):
        moved = moving(turn)
        for a in range(3):
            for b in range(3):
                for core in range(2):
                    go((moved[0][(a + b) % 3], fixed[1][(2, 1, 3)[a]], fixed[2][(2, 1, 3)[b]]), core)
        return carry

    def two_axes(turn, carry):
        moved = moving(turn)
        for a in range(3):
            for still in range(3):
                place = [at for at in here]
                place[(still + 1) % 3] = fixed[(still + 1) % 3][(2, 1, 3)[a]]
                place[(still + 2) % 3] = moved[(still + 2) % 3][(a + still) % 3]
                for core in range(2):
                    go(place, core)
        return carry

    def one_axis(turn, carry):
        moved = moving(turn)
        for axis in range(3):
            place = [at for at in here]
            place[axis] = moved[axis][axis]
            for core in range(2):
                go(place, core)
        return carry

    for walk in (three_axes, two_axes, one_axis):
        lax.fori_loop(0, 3, walk, 0)
    go(here, 1)


def kernel(
    q_hbm, k_hbm, v_hbm, h_hbm, gain_hbm, fo_hbm, fi_hbm, ii_hbm, io_hbm, tw_hbm, out_hbm,
    q_buf, k_buf, v_buf, h_buf, gain_buf, fo_buf, fi_buf, ii_buf, io_buf, tw_buf, out_buf,
    send, recv, wide, tap_spec, ywide, ysend, yrecv,
    in_sem, out_sem, send_sem, recv_sem, ysend_sem, yrecv_sem,
):
    seq, chan = lax.axis_index("seq"), lax.axis_index("chan")
    me = seq * 16 + chan

    pairs = (
        (h_hbm, h_buf), (k_hbm, k_buf), (v_hbm, v_buf), (fo_hbm, fo_buf), (fi_hbm, fi_buf), (ii_hbm, ii_buf),
        (io_hbm, io_buf), (tw_hbm, tw_buf), (q_hbm, q_buf), (gain_hbm, gain_buf),
    )
    loads = [pltpu.make_async_copy(src, dst, in_sem.at[i]) for i, (src, dst) in enumerate(pairs)]
    for load in loads:
        load.start()

    barrier = pltpu.get_barrier_semaphore()
    sweep(lambda peer, place: pl.semaphore_signal(barrier, inc=1, device_id=place, device_id_type=MESH))

    def lanes_of(chunk, block):
        return pl.ds(pl.multiple_of(chunk * (BLOCKS * 128) + block * 128, 128), 128)

    def pack_taps(chunk, block, carry):
        send[chunk, pl.ds(block * 8, 8)] = h_buf[:, lanes_of(chunk, block)].T.reshape(8, CC, TOK)
        return carry

    def pack_product(chunk, block, carry):
        lanes = lanes_of(chunk, block)
        product = (k_buf[:, lanes].astype(F32) * v_buf[:, lanes].astype(F32)).astype(BF16)
        send[CHUNKS + chunk, pl.ds(block * 8, 8)] = product.T.reshape(8, CC, TOK)
        return carry

    def give(piece):
        def visit(peer, place):
            pltpu.make_async_remote_copy(
                src_ref=send.at[piece, peer], dst_ref=recv.at[piece, me],
                send_sem=send_sem.at[piece], recv_sem=recv_sem.at[piece],
                device_id=place, device_id_type=MESH,
            ).start()

        sweep(visit)
        recv[piece, me] = send[piece, me]

    loads[0].wait()
    for chunk in range(CHUNKS):
        lax.fori_loop(0, BLOCKS, functools.partial(pack_taps, chunk), 0, unroll=UNROLL)
    loads[1].wait()
    loads[2].wait()
    lax.fori_loop(0, BLOCKS, functools.partial(pack_product, 0), 0, unroll=UNROLL)
    pl.semaphore_wait(barrier, DEVS - 1)
    for piece in range(CHUNKS + 1):
        give(piece)
    lax.fori_loop(0, BLOCKS, functools.partial(pack_product, 1), 0, unroll=UNROLL)
    give(CHUNKS + 1)
    for load in loads[3:]:
        load.wait()

    others = pl.ds(0, DEVS - 1)

    def widen(piece, step, carry):
        rows = pl.ds(pl.multiple_of(step * (16 * CC), 16 * CC), 16 * CC)
        wide[rows, :] = recv[piece, pl.ds(step * 16, 16)].reshape(16 * CC, TOK).astype(F32)
        return carry

    def spectra(first):
        twist_re, twist_im = tw_buf[0], tw_buf[1]
        rows = []
        for c in range(0, BATCH, 2):
            both = jnp.concatenate(
                [wide[pl.ds(first + c + odd, DEVS, CC), :].astype(BF16) for odd in range(2)], axis=1)
            both = jnp.dot(fo_buf[...], both, preferred_element_type=F32)
            for lane in (0, 128):
                re, im = both[:128, lane:lane + 128], both[128:, lane:lane + 128]
                rows.append(jnp.concatenate(
                    [(re * twist_re - im * twist_im).astype(BF16), (re * twist_im + im * twist_re).astype(BF16)], axis=1))
        return jnp.dot(jnp.concatenate(rows, axis=0), fi_buf[...], preferred_element_type=F32)

    def transform_taps(chunk, at, carry):
        rows = pl.ds(pl.multiple_of((chunk * CC + at * BATCH) * 128, 128), BATCH * 128)
        tap_spec[rows, :] = spectra(at * BATCH)
        return carry

    def convolve(chunk, at, carry):
        twist_re, twist_im = tw_buf[0], tw_buf[1]
        x_all = spectra(at * BATCH)
        products = []
        for c in range(BATCH):
            taps = tap_spec[pl.ds(pl.multiple_of((chunk * CC + at * BATCH + c) * 128, 128), 128), :]
            x_re, x_im = x_all[c * 128:c * 128 + 128, :128], x_all[c * 128:c * 128 + 128, 128:]
            h_re, h_im = taps[:, :128], taps[:, 128:]
            products.append(jnp.concatenate(
                [(x_re * h_re - x_im * h_im).astype(BF16), (x_re * h_im + x_im * h_re).astype(BF16)], axis=1))
        back = jnp.dot(jnp.concatenate(products, axis=0), ii_buf[...], preferred_element_type=F32)
        turned = []
        for c in range(BATCH):
            re, im = back[c * 128:c * 128 + 128, :128], back[c * 128:c * 128 + 128, 128:]
            turned.append(jnp.concatenate(
                [(re * twist_re + im * twist_im).astype(BF16), (im * twist_re - re * twist_im).astype(BF16)], axis=0))
        for c in range(0, BATCH, 2):
            y = jnp.dot(io_buf[...], jnp.concatenate(turned[c:c + 2], axis=1), preferred_element_type=F32)
            ywide[pl.ds(BATCH * at + c, DEVS, CC), :] = y[:, :128]
            ywide[pl.ds(BATCH * at + c + 1, DEVS, CC), :] = y[:, 128:]
        return carry

    def narrow(chunk, step, carry):
        rows = pl.ds(pl.multiple_of(step * (16 * CC), 16 * CC), 16 * CC)
        ysend[chunk, pl.ds(step * 16, 16)] = ywide[rows, :].astype(BF16).reshape(16, CC, TOK)
        return carry

    def give_back(chunk):
        def visit(peer, place):
            pltpu.make_async_remote_copy(
                src_ref=ysend.at[chunk, peer], dst_ref=yrecv.at[chunk, me],
                send_sem=ysend_sem.at[chunk], recv_sem=yrecv_sem.at[chunk],
                device_id=place, device_id_type=MESH,
            ).start()

        sweep(visit)
        yrecv[chunk, me] = ysend[chunk, me]

    for piece in range(2 * CHUNKS):
        chunk = piece % CHUNKS
        arrived = recv.at[piece, others]
        pltpu.make_async_copy(arrived, arrived, recv_sem.at[piece]).wait()
        lax.fori_loop(0, 8, functools.partial(widen, piece), 0)
        if piece < CHUNKS:
            lax.fori_loop(0, CC // BATCH, functools.partial(transform_taps, chunk), 0)
        else:
            lax.fori_loop(0, CC // BATCH, functools.partial(convolve, chunk), 0)
            lax.fori_loop(0, 8, functools.partial(narrow, chunk), 0)
            give_back(chunk)

    def gate(chunk, block, carry):
        lanes = lanes_of(chunk, block)
        convolved = yrecv[chunk, pl.ds(block * 8, 8)].reshape(128, TOK).T.astype(F32)
        product = (k_buf[:, lanes].astype(F32) * v_buf[:, lanes].astype(F32)).astype(BF16).astype(F32)
        out_buf[:, lanes] = (q_buf[:, lanes].astype(F32) * (convolved + gain_buf[:, lanes] * product)).astype(BF16)
        return carry

    stores = []
    for chunk in range(CHUNKS):
        arrived = yrecv.at[chunk, others]
        pltpu.make_async_copy(arrived, arrived, yrecv_sem.at[chunk]).wait()
        lax.fori_loop(0, BLOCKS, functools.partial(gate, chunk), 0, unroll=UNROLL)
        half = pl.ds(chunk * BLOCKS * 128, BLOCKS * 128)
        stores.append(pltpu.make_async_copy(out_buf.at[:, half], out_hbm.at[:, half], out_sem.at[chunk]))
        stores[-1].start()
    for store in stores:
        store.wait()
    for piece in range(2 * CHUNKS):
        left = send.at[piece, others]
        pltpu.make_async_copy(left, left, send_sem.at[piece]).wait()
    for chunk in range(CHUNKS):
        left = ysend.at[chunk, others]
        pltpu.make_async_copy(left, left, ysend_sem.at[chunk]).wait()


def shards(query_proj, key_proj, value_proj, filter_taps, skip_gain):
    whole = (TOK, 4096)
    any_spec = pl.BlockSpec(memory_space=pltpu.HBM)
    return pl.pallas_call(
        kernel,
        out_shape=jax.ShapeDtypeStruct(whole, BF16),
        in_specs=[any_spec] * 10,
        out_specs=pl.BlockSpec(memory_space=pl.ANY),
        scratch_shapes=[
            pltpu.VMEM(whole, BF16), pltpu.VMEM(whole, BF16), pltpu.VMEM(whole, BF16), pltpu.VMEM(whole, BF16),
            pltpu.VMEM((1, 4096), F32),
            pltpu.VMEM((256, 128), BF16), pltpu.VMEM((256, 256), BF16), pltpu.VMEM((256, 256), BF16),
            pltpu.VMEM((128, 256), BF16), pltpu.VMEM((2, 128, 128), F32),
            pltpu.VMEM(whole, BF16),
            pltpu.VMEM((2 * CHUNKS, DEVS, CC, TOK), BF16), pltpu.VMEM((2 * CHUNKS, DEVS, CC, TOK), BF16),
            pltpu.VMEM((DEVS * CC, TOK), F32), pltpu.VMEM((CHUNKS * CC * 128, 256), F32), pltpu.VMEM((DEVS * CC, TOK), F32),
            pltpu.VMEM((CHUNKS, DEVS, CC, TOK), BF16), pltpu.VMEM((CHUNKS, DEVS, CC, TOK), BF16),
            pltpu.SemaphoreType.DMA((10,)), pltpu.SemaphoreType.DMA((CHUNKS,)),
            pltpu.SemaphoreType.DMA((2 * CHUNKS,)), pltpu.SemaphoreType.DMA((2 * CHUNKS,)),
            pltpu.SemaphoreType.DMA((CHUNKS,)), pltpu.SemaphoreType.DMA((CHUNKS,)),
        ],
        compiler_params=pltpu.CompilerParams(
            collective_id=0, has_side_effects=True, vmem_limit_bytes=60 << 20
        ),
        cost_estimate=pl.CostEstimate(flops=3 << 30, bytes_accessed=6 << 20, transcendentals=0),
        name="long_conv",
    )(query_proj, key_proj, value_proj, filter_taps, skip_gain.reshape(1, 4096), *(jnp.asarray(t) for t in tables()))


def solution(mesh):
    split = P(("seq", "chan"), None)
    return jax.shard_map(
        shards, mesh=mesh, in_specs=(split, split, split, split, P()), out_specs=split, check_vma=False
    )
```

time: 70.8 us -> 54.5 us (0.77)
  Pallas kernels: 68.1 us -> 52 us
    pallas_call x1, Pallas kernels: 68.1 us -> 52 us  [shards(): pl.pallas_call(kernel, out_shape=jax.ShapeDtypeStruct(whole, BF16), in_sp...]
where the time goes in v1:
time: 54.5 us; the launch traced here: 54.3 us
  Pallas kernels  52 us (95%)
  local copies, waits for them, and re-layouts  2.29 us (4%)
    pallas_call x1, Pallas kernels, shards(): pl.pallas_call(kernel, out_shape=jax.ShapeDtypeStruct(whole, BF16), in_sp...  52 us
    unnamed x1, local copies, waits for them, and re-layouts  2.29 us

profile of v1, /device:TPU:1, one launch (start us, length us, event | category | flops | bytes accessed | tf_op | source)
XLA Modules:
  0.0 54.3 jit_solution(11389509662793446401)
XLA Ops:
  0.0 52.0 %long_conv.1 = bf16[128,4096]{1,0:T(8,128)(2,1)} custom-call(bf16[128,4096]{1,0:T(8,128)(2,1)} %q_hbm.1, bf16[128,4096]{1,0:T(8,128)(2,1)} %k_hbm.1, bf16[128,4096]{1,0:T(8,128)(2,1)} %v_hbm.1, bf16[128,4096]{1,0:T(8,128)(2,1)} %h_hbm.1, f32[1,4096]{1,0:T(1,128)} %bitcast.1, bf16[256,128]{1,0:T(8,128)(2,1)} %constant.10.clone.fo_hbm, ...), custom_call_target="tpu_custom_call" | custom-call | flops 3221225472 | bytes 6291456 | tf_op jit(solution)/shard_map/long_conv/pallas_call | solution.py:252
  52.0 2.3 %copy.12 = bf16[128,4096]{1,0:T(8,128)(2,1)} copy(bf16[128,4096]{1,0:T(8,128)(2,1)} %long_conv.1) | data formatting | bytes 2097152

commit v2 on v1

--- a/solution.py
+++ b/solution.py
@@ -41,58 +41,34 @@
     )
 
 
+STEPS = (
+    84, 85, 86, 116, 77, 52, 87, 76, 93, 117, 83, 53, 92, 82, 45, 54,
+    74, 91, 20, 95, 60, 75, 55, 109, 119, 79, 61, 115, 90, 124, 80, 125,
+    118, 94, 44, 78, 21, 81, 108, 69, 114, 50, 68, 51, 42, 122, 43, 111,
+    123, 63, 106, 62, 59, 46, 107, 126, 58, 47, 127, 110, 12, 72, 22, 70,
+    13, 73, 101, 112, 19, 67, 18, 71, 29, 88, 49, 36, 28, 89, 66, 23,
+    48, 100, 113, 37, 15, 102, 121, 98, 27, 120, 30, 40, 39, 99, 104, 31,
+    38, 105, 14, 103, 11, 41, 34, 17, 35, 56, 10, 5, 64, 57, 26, 16,
+    4, 65, 97, 9, 7, 8, 96, 3, 6, 25, 32, 2, 24, 33, 1,
+)
+
+
 def sweep(visit):
     seq, chan = lax.axis_index("seq"), lax.axis_index("chan")
-    here = (chan // 4, seq // 2, chan % 4)
+    sense = 1 + 2 * (seq % 2)
+    x, y, z = ([lax.rem(at + far * sense, 4) for far in range(4)] for at in (chan // 4, seq // 2, chan % 4))
     cores = (seq % 2, 1 - seq % 2)
-    fixed = [[lax.rem(at + far, 4) for far in range(4)] for at in here]
-
-    def go(place, core):
-        seq_to, chan_to = place[1] * 2 + cores[core], place[0] * 4 + place[2]
+    for code in STEPS:
+        seq_to = y[code // 8 % 4] * 2 + cores[code % 2]
+        chan_to = x[code // 32] * 4 + z[code // 2 % 4]
         visit(seq_to * 16 + chan_to, (seq_to, chan_to))
 
-    def moving(turn):
-        fars = (turn + 1, lax.rem(turn + 1, 3) + 1, lax.rem(turn + 2, 3) + 1)
-        return [[lax.rem(at + far, 4) for far in fars] for at in here]
-
-    def three_axes(turn, carry):
-        moved = moving(turn)
-        for a in range(3):
-            for b in range(3):
-                for core in range(2):
-                    go((moved[0][(a + b) % 3], fixed[1][(2, 1, 3)[a]], fixed[2][(2, 1, 3)[b]]), core)
-        return carry
-
-    def two_axes(turn, carry):
-        moved = moving(turn)
-        for a in range(3):
-            for still in range(3):
-                place = [at for at in here]
-                place[(still + 1) % 3] = fixed[(still + 1) % 3][(2, 1, 3)[a]]
-                place[(still + 2) % 3] = moved[(still + 2) % 3][(a + still) % 3]
-                for core in range(2):
-                    go(place, core)
-        return carry
-
-    def one_axis(turn, carry):
-        moved = moving(turn)
-        for axis in range(3):
-            place = [at for at in here]
-            place[axis] = moved[axis][axis]
-            for core in range(2):
-                go(place, core)
-        return carry
-
-    for walk in (three_axes, two_axes, one_axis):
-        lax.fori_loop(0, 3, walk, 0)
-    go(here, 1)
-
 
 def kernel(
-    q_hbm, k_hbm, v_hbm, h_hbm, gain_hbm, fo_hbm, fi_hbm, ii_hbm, io_hbm, tw_hbm, out_hbm,
-    q_buf, k_buf, v_buf, h_buf, gain_buf, fo_buf, fi_buf, ii_buf, io_buf, tw_buf, out_buf,
+    q_hbm, k_hbm, v_hbm, h_hbm, gain_hbm, fo_hbm, fi_hbm, ii_hbm, io_hbm, tw_hbm, out_buf,
+    q_buf, k_buf, v_buf, h_buf, gain_buf, fo_buf, fi_buf, ii_buf, io_buf, tw_buf,
     send, recv, wide, tap_spec, ywide, ysend, yrecv,
-    in_sem, out_sem, send_sem, recv_sem, ysend_sem, yrecv_sem,
+    in_sem, send_sem, recv_sem, ysend_sem, yrecv_sem,
 ):
     seq, chan = lax.axis_index("seq"), lax.axis_index("chan")
     me = seq * 16 + chan
@@ -130,19 +106,23 @@
             ).start()
 
         sweep(visit)
-        recv[piece, me] = send[piece, me]
 
     loads[0].wait()
     for chunk in range(CHUNKS):
         lax.fori_loop(0, BLOCKS, functools.partial(pack_taps, chunk), 0, unroll=UNROLL)
+    pl.semaphore_wait(barrier, DEVS - 1)
     loads[1].wait()
     loads[2].wait()
     lax.fori_loop(0, BLOCKS, functools.partial(pack_product, 0), 0, unroll=UNROLL)
-    pl.semaphore_wait(barrier, DEVS - 1)
-    for piece in range(CHUNKS + 1):
+
+    @pl.loop(0, CHUNKS + 1)
+    def _(piece):
         give(piece)
+
     lax.fori_loop(0, BLOCKS, functools.partial(pack_product, 1), 0, unroll=UNROLL)
     give(CHUNKS + 1)
+    for piece in range(2 * CHUNKS):
+        recv[piece, me] = send[piece, me]
     for load in loads[3:]:
         load.wait()
 
@@ -209,17 +189,22 @@
         sweep(visit)
         yrecv[chunk, me] = ysend[chunk, me]
 
-    for piece in range(2 * CHUNKS):
-        chunk = piece % CHUNKS
+    def take(piece):
         arrived = recv.at[piece, others]
         pltpu.make_async_copy(arrived, arrived, recv_sem.at[piece]).wait()
         lax.fori_loop(0, 8, functools.partial(widen, piece), 0)
-        if piece < CHUNKS:
-            lax.fori_loop(0, CC // BATCH, functools.partial(transform_taps, chunk), 0)
-        else:
-            lax.fori_loop(0, CC // BATCH, functools.partial(convolve, chunk), 0)
-            lax.fori_loop(0, 8, functools.partial(narrow, chunk), 0)
-            give_back(chunk)
+
+    @pl.loop(0, CHUNKS)
+    def _(chunk):
+        take(chunk)
+        lax.fori_loop(0, CC // BATCH, functools.partial(transform_taps, chunk), 0)
+
+    @pl.loop(0, CHUNKS)
+    def _(chunk):
+        take(CHUNKS + chunk)
+        lax.fori_loop(0, CC // BATCH, functools.partial(convolve, chunk), 0)
+        lax.fori_loop(0, 8, functools.partial(narrow, chunk), 0)
+        give_back(chunk)
 
     def gate(chunk, block, carry):
         lanes = lanes_of(chunk, block)
@@ -228,16 +213,10 @@
         out_buf[:, lanes] = (q_buf[:, lanes].astype(F32) * (convolved + gain_buf[:, lanes] * product)).astype(BF16)
         return carry
 
-    stores = []
     for chunk in range(CHUNKS):
         arrived = yrecv.at[chunk, others]
         pltpu.make_async_copy(arrived, arrived, yrecv_sem.at[chunk]).wait()
         lax.fori_loop(0, BLOCKS, functools.partial(gate, chunk), 0, unroll=UNROLL)
-        half = pl.ds(chunk * BLOCKS * 128, BLOCKS * 128)
-        stores.append(pltpu.make_async_copy(out_buf.at[:, half], out_hbm.at[:, half], out_sem.at[chunk]))
-        stores[-1].start()
-    for store in stores:
-        store.wait()
     for piece in range(2 * CHUNKS):
         left = send.at[piece, others]
         pltpu.make_async_copy(left, left, send_sem.at[piece]).wait()
@@ -248,31 +227,33 @@
 
 def shards(query_proj, key_proj, value_proj, filter_taps, skip_gain):
     whole = (TOK, 4096)
-    any_spec = pl.BlockSpec(memory_space=pltpu.HBM)
+    held = [
+        pltpu.with_memory_space_constraint(a, pltpu.HBM)
+        for a in (query_proj, key_proj, value_proj, filter_taps, skip_gain.reshape(1, 4096), *map(jnp.asarray, tables()))
+    ]
     return pl.pallas_call(
         kernel,
-        out_shape=jax.ShapeDtypeStruct(whole, BF16),
-        in_specs=[any_spec] * 10,
-        out_specs=pl.BlockSpec(memory_space=pl.ANY),
+        out_shape=pltpu.VMEM(whole, BF16),
+        in_specs=[pl.BlockSpec(memory_space=pltpu.HBM)] * len(held),
+        out_specs=pl.BlockSpec(memory_space=pltpu.VMEM),
         scratch_shapes=[
             pltpu.VMEM(whole, BF16), pltpu.VMEM(whole, BF16), pltpu.VMEM(whole, BF16), pltpu.VMEM(whole, BF16),
             pltpu.VMEM((1, 4096), F32),
             pltpu.VMEM((256, 128), BF16), pltpu.VMEM((256, 256), BF16), pltpu.VMEM((256, 256), BF16),
             pltpu.VMEM((128, 256), BF16), pltpu.VMEM((2, 128, 128), F32),
-            pltpu.VMEM(whole, BF16),
             pltpu.VMEM((2 * CHUNKS, DEVS, CC, TOK), BF16), pltpu.VMEM((2 * CHUNKS, DEVS, CC, TOK), BF16),
             pltpu.VMEM((DEVS * CC, TOK), F32), pltpu.VMEM((CHUNKS * CC * 128, 256), F32), pltpu.VMEM((DEVS * CC, TOK), F32),
             pltpu.VMEM((CHUNKS, DEVS, CC, TOK), BF16), pltpu.VMEM((CHUNKS, DEVS, CC, TOK), BF16),
-            pltpu.SemaphoreType.DMA((10,)), pltpu.SemaphoreType.DMA((CHUNKS,)),
+            pltpu.SemaphoreType.DMA((10,)),
             pltpu.SemaphoreType.DMA((2 * CHUNKS,)), pltpu.SemaphoreType.DMA((2 * CHUNKS,)),
             pltpu.SemaphoreType.DMA((CHUNKS,)), pltpu.SemaphoreType.DMA((CHUNKS,)),
         ],
         compiler_params=pltpu.CompilerParams(
-            collective_id=0, has_side_effects=True, vmem_limit_bytes=60 << 20
+            collective_id=0, has_side_effects=True, vmem_limit_bytes=48 << 20
         ),
         cost_estimate=pl.CostEstimate(flops=3 << 30, bytes_accessed=6 << 20, transcendentals=0),
         name="long_conv",
-    )(query_proj, key_proj, value_proj, filter_taps, skip_gain.reshape(1, 4096), *(jnp.asarray(t) for t in tables()))
+    )(*held)
 
 
 def solution(mesh):

time: 54.5 us -> 49.8 us (0.914)
  Pallas kernels: 52 us -> 48.7 us
  local copies, waits for them, and re-layouts: 2.29 us -> 0.97 us
    pallas_call x1, Pallas kernels: 52 us -> 48.7 us  [shards(): pl.pallas_call(kernel, out_shape=pltpu.VMEM(whole, BF16), in_specs=[pl.Bl...]
    unnamed x1, local copies, waits for them, and re-layouts: 2.29 us -> 0.97 us
where the time goes in v2:
time: 49.8 us; the launch traced here: 49.7 us
  Pallas kernels  48.7 us (98%)
  local copies, waits for them, and re-layouts  0.97 us (2%)
    pallas_call x1, Pallas kernels, shards(): pl.pallas_call(kernel, out_shape=pltpu.VMEM(whole, BF16), in_specs=[pl.Bl...  48.7 us

profile of v2, /device:TPU:1, one launch (start us, length us, event | category | flops | bytes accessed | tf_op | source)
XLA Modules:
  0.0 49.7 jit_solution(6686358641231441441)
XLA Ops:
  0.0 48.7 %long_conv.1 = bf16[128,4096]{1,0:T(8,128)(2,1)S(1)} custom-call(bf16[128,4096]{1,0:T(8,128)(2,1)} %q_hbm.1, bf16[128,4096]{1,0:T(8,128)(2,1)} %k_hbm.1, bf16[128,4096]{1,0:T(8,128)(2,1)} %v_hbm.1, bf16[128,4096]{1,0:T(8,128)(2,1)} %h_hbm.1, f32[1,4096]{1,0:T(1,128)} %bitcast.1, bf16[256,128]{1,0:T(8,128)(2,1)} %constant.10.clone.fo_hbm, ...), custom_call_target="tpu_custom_call" | custom-call | flops 3221225472 | bytes 6291456 | tf_op jit(solution)/shard_map/long_conv/pallas_call | solution.py:234
  48.7 1.0 %copy.12 = bf16[128,4096]{1,0:T(8,128)(2,1)} copy(bf16[128,4096]{1,0:T(8,128)(2,1)S(1)} %long_conv.1) | data formatting | bytes 2097152

commit v3 on v2

--- a/solution.py
+++ b/solution.py
@@ -78,8 +78,13 @@
         (io_hbm, io_buf), (tw_hbm, tw_buf), (q_hbm, q_buf), (gain_hbm, gain_buf),
     )
     loads = [pltpu.make_async_copy(src, dst, in_sem.at[i]) for i, (src, dst) in enumerate(pairs)]
-    for load in loads:
-        load.start()
+    for i, load in enumerate(loads):
+        if i < 3:
+            for part in range(4):
+                rows = pl.ds(part * (TOK // 4), TOK // 4)
+                pltpu.make_async_copy(pairs[i][0].at[rows], pairs[i][1].at[rows], in_sem.at[i]).start()
+        else:
+            load.start()
 
     barrier = pltpu.get_barrier_semaphore()
     sweep(lambda peer, place: pl.semaphore_signal(barrier, inc=1, device_id=place, device_id_type=MESH))
@@ -107,20 +112,30 @@
 
         sweep(visit)
 
+    def pack(body):
+        lax.fori_loop(0, BLOCKS, body, 0, unroll=UNROLL)
+
     loads[0].wait()
-    for chunk in range(CHUNKS):
-        lax.fori_loop(0, BLOCKS, functools.partial(pack_taps, chunk), 0, unroll=UNROLL)
+    pack(functools.partial(pack_taps, 0))
     pl.semaphore_wait(barrier, DEVS - 1)
-    loads[1].wait()
-    loads[2].wait()
-    lax.fori_loop(0, BLOCKS, functools.partial(pack_product, 0), 0, unroll=UNROLL)
-
-    @pl.loop(0, CHUNKS + 1)
+
+    @pl.loop(0, 2 * CHUNKS)
     def _(piece):
+        @pl.when(piece == 1)
+        def _():
+            pack(functools.partial(pack_taps, 1))
+
+        @pl.when(piece == CHUNKS)
+        def _():
+            loads[1].wait()
+            loads[2].wait()
+
+        @pl.when(piece >= CHUNKS)
+        def _():
+            pack(functools.partial(pack_product, piece - CHUNKS))
+
         give(piece)
 
-    lax.fori_loop(0, BLOCKS, functools.partial(pack_product, 1), 0, unroll=UNROLL)
-    give(CHUNKS + 1)
     for piece in range(2 * CHUNKS):
         recv[piece, me] = send[piece, me]
     for load in loads[3:]:
@@ -242,7 +257,7 @@
             pltpu.VMEM((256, 128), BF16), pltpu.VMEM((256, 256), BF16), pltpu.VMEM((256, 256), BF16),
             pltpu.VMEM((128, 256), BF16), pltpu.VMEM((2, 128, 128), F32),
             pltpu.VMEM((2 * CHUNKS, DEVS, CC, TOK), BF16), pltpu.VMEM((2 * CHUNKS, DEVS, CC, TOK), BF16),
-            pltpu.VMEM((DEVS * CC, TOK), F32), pltpu.VMEM((CHUNKS * CC * 128, 256), F32), pltpu.VMEM((DEVS * CC, TOK), F32),
+            pltpu.VMEM((DEVS * CC + CC, TOK), F32), pltpu.VMEM((CHUNKS * CC * 128, 256), F32), pltpu.VMEM((DEVS * CC + CC, TOK), F32),
             pltpu.VMEM((CHUNKS, DEVS, CC, TOK), BF16), pltpu.VMEM((CHUNKS, DEVS, CC, TOK), BF16),
             pltpu.SemaphoreType.DMA((10,)),
             pltpu.SemaphoreType.DMA((2 * CHUNKS,)), pltpu.SemaphoreType.DMA((2 * CHUNKS,)),

time: 49.8 us -> 49.3 us (0.990)
  Pallas kernels: 48.7 us -> 48.2 us
    pallas_call x1, Pallas kernels: 48.7 us -> 48.2 us  [shards(): pl.pallas_call(kernel, out_shape=pltpu.VMEM(whole, BF16), in_specs=[pl.Bl...]
where the time goes in v3:
time: 49.3 us; the launch traced here: 49.2 us
  Pallas kernels  48.2 us (98%)
  local copies, waits for them, and re-layouts  0.97 us (2%)
    pallas_call x1, Pallas kernels, shards(): pl.pallas_call(kernel, out_shape=pltpu.VMEM(whole, BF16), in_specs=[pl.Bl...  48.2 us

profile of v3, /device:TPU:1, one launch (start us, length us, event | category | flops | bytes accessed | tf_op | source)
XLA Modules:
  0.0 49.2 jit_solution(12980330979867586724)
XLA Ops:
  0.0 48.2 %long_conv.1 = bf16[128,4096]{1,0:T(8,128)(2,1)S(1)} custom-call(bf16[128,4096]{1,0:T(8,128)(2,1)} %q_hbm.1, bf16[128,4096]{1,0:T(8,128)(2,1)} %k_hbm.1, bf16[128,4096]{1,0:T(8,128)(2,1)} %v_hbm.1, bf16[128,4096]{1,0:T(8,128)(2,1)} %h_hbm.1, f32[1,4096]{1,0:T(1,128)} %bitcast.1, bf16[256,128]{1,0:T(8,128)(2,1)} %constant.10.clone.fo_hbm, ...), custom_call_target="tpu_custom_call" | custom-call | flops 3221225472 | bytes 6291456 | tf_op jit(solution)/shard_map/long_conv/pallas_call | solution.py:249
  48.2 1.0 %copy.12 = bf16[128,4096]{1,0:T(8,128)(2,1)} copy(bf16[128,4096]{1,0:T(8,128)(2,1)S(1)} %long_conv.1) | data formatting | bytes 2097152

commit v4 on v3

--- a/solution.py
+++ b/solution.py
@@ -78,16 +78,19 @@
         (io_hbm, io_buf), (tw_hbm, tw_buf), (q_hbm, q_buf), (gain_hbm, gain_buf),
     )
     loads = [pltpu.make_async_copy(src, dst, in_sem.at[i]) for i, (src, dst) in enumerate(pairs)]
-    for i, load in enumerate(loads):
-        if i < 3:
-            for part in range(4):
-                rows = pl.ds(part * (TOK // 4), TOK // 4)
-                pltpu.make_async_copy(pairs[i][0].at[rows], pairs[i][1].at[rows], in_sem.at[i]).start()
-        else:
-            load.start()
-
+
+    def load_parts(i):
+        for part in range(4):
+            rows = pl.ds(part * (TOK // 4), TOK // 4)
+            pltpu.make_async_copy(pairs[i][0].at[rows], pairs[i][1].at[rows], in_sem.at[i]).start()
+
+    load_parts(0)
     barrier = pltpu.get_barrier_semaphore()
     sweep(lambda peer, place: pl.semaphore_signal(barrier, inc=1, device_id=place, device_id_type=MESH))
+    for i in (1, 2):
+        load_parts(i)
+    for load in loads[3:]:
+        load.start()
 
     def lanes_of(chunk, block):
         return pl.ds(pl.multiple_of(chunk * (BLOCKS * 128) + block * 128, 128), 128)
@@ -197,12 +200,12 @@
         def visit(peer, place):
             pltpu.make_async_remote_copy(
                 src_ref=ysend.at[chunk, peer], dst_ref=yrecv.at[chunk, me],
-                send_sem=ysend_sem.at[chunk], recv_sem=yrecv_sem.at[chunk],
+                send_sem=ysend_sem.at[chunk], recv_sem=yrecv_sem.at[chunk, me // 32],
                 device_id=place, device_id_type=MESH,
             ).start()
 
         sweep(visit)
-        yrecv[chunk, me] = ysend[chunk, me]
+        pltpu.make_async_copy(ysend.at[chunk, me], yrecv.at[chunk, me], yrecv_sem.at[chunk, me // 32]).start()
 
     def take(piece):
         arrived = recv.at[piece, others]
@@ -229,9 +232,12 @@
         return carry
 
     for chunk in range(CHUNKS):
-        arrived = yrecv.at[chunk, others]
-        pltpu.make_async_copy(arrived, arrived, yrecv_sem.at[chunk]).wait()
-        lax.fori_loop(0, BLOCKS, functools.partial(gate, chunk), 0, unroll=UNROLL)
+        for ahead in (2, 1, 3, 0):
+            quarter = lax.rem(me // 32 + ahead, 4)
+            arrived = yrecv.at[chunk, pl.ds(quarter * 32, 32)]
+            pltpu.make_async_copy(arrived, arrived, yrecv_sem.at[chunk, quarter]).wait()
+            for block in range(4):
+                gate(chunk, quarter * 4 + block, 0)
     for piece in range(2 * CHUNKS):
         left = send.at[piece, others]
         pltpu.make_async_copy(left, left, send_sem.at[piece]).wait()
@@ -261,7 +267,7 @@
             pltpu.VMEM((CHUNKS, DEVS, CC, TOK), BF16), pltpu.VMEM((CHUNKS, DEVS, CC, TOK), BF16),
             pltpu.SemaphoreType.DMA((10,)),
             pltpu.SemaphoreType.DMA((2 * CHUNKS,)), pltpu.SemaphoreType.DMA((2 * CHUNKS,)),
-            pltpu.SemaphoreType.DMA((CHUNKS,)), pltpu.SemaphoreType.DMA((CHUNKS,)),
+            pltpu.SemaphoreType.DMA((CHUNKS,)), pltpu.SemaphoreType.DMA((CHUNKS, 4)),
         ],
         compiler_params=pltpu.CompilerParams(
             collective_id=0, has_side_effects=True, vmem_limit_bytes=48 << 20

time: 49.3 us -> 49 us (level)
  no operation moved by 1% of the time
where the time goes in v4:
time: 49 us; the launch traced here: 48.9 us
  Pallas kernels  47.9 us (98%)
  local copies, waits for them, and re-layouts  0.97 us (2%)
    pallas_call x1, Pallas kernels, shards(): pl.pallas_call(kernel, out_shape=pltpu.VMEM(whole, BF16), in_specs=[pl.Bl...  47.9 us

profile of v4, /device:TPU:1, one launch (start us, length us, event | category | flops | bytes accessed | tf_op | source)
XLA Modules:
  0.0 48.9 jit_solution(7372694959572112221)
XLA Ops:
  0.0 47.9 %long_conv.1 = bf16[128,4096]{1,0:T(8,128)(2,1)S(1)} custom-call(bf16[128,4096]{1,0:T(8,128)(2,1)} %q_hbm.1, bf16[128,4096]{1,0:T(8,128)(2,1)} %k_hbm.1, bf16[128,4096]{1,0:T(8,128)(2,1)} %v_hbm.1, bf16[128,4096]{1,0:T(8,128)(2,1)} %h_hbm.1, f32[1,4096]{1,0:T(1,128)} %bitcast.1, bf16[256,128]{1,0:T(8,128)(2,1)} %constant.10.clone.fo_hbm, ...), custom_call_target="tpu_custom_call" | custom-call | flops 3221225472 | bytes 6291456 | tf_op jit(solution)/shard_map/long_conv/pallas_call | solution.py:255
  47.9 1.0 %copy.12 = bf16[128,4096]{1,0:T(8,128)(2,1)} copy(bf16[128,4096]{1,0:T(8,128)(2,1)S(1)} %long_conv.1) | data formatting | bytes 2097152

commit v5 on v4

--- a/solution.py
+++ b/solution.py
@@ -84,10 +84,9 @@
             rows = pl.ds(part * (TOK // 4), TOK // 4)
             pltpu.make_async_copy(pairs[i][0].at[rows], pairs[i][1].at[rows], in_sem.at[i]).start()
 
-    load_parts(0)
     barrier = pltpu.get_barrier_semaphore()
     sweep(lambda peer, place: pl.semaphore_signal(barrier, inc=1, device_id=place, device_id_type=MESH))
-    for i in (1, 2):
+    for i in range(3):
         load_parts(i)
     for load in loads[3:]:
         load.start()

time: 49 us -> 48.7 us (level)
  no operation moved by 1% of the time
where the time goes in v5:
time: 48.7 us; the launch traced here: 48.6 us
  Pallas kernels  47.6 us (98%)
  local copies, waits for them, and re-layouts  0.97 us (2%)
    pallas_call x1, Pallas kernels, shards(): pl.pallas_call(kernel, out_shape=pltpu.VMEM(whole, BF16), in_specs=[pl.Bl...  47.6 us

profile of v5, /device:TPU:1, one launch (start us, length us, event | category | flops | bytes accessed | tf_op | source)
XLA Modules:
  0.0 48.6 jit_solution(14913124530284250063)
XLA Ops:
  0.0 47.6 %long_conv.1 = bf16[128,4096]{1,0:T(8,128)(2,1)S(1)} custom-call(bf16[128,4096]{1,0:T(8,128)(2,1)} %q_hbm.1, bf16[128,4096]{1,0:T(8,128)(2,1)} %k_hbm.1, bf16[128,4096]{1,0:T(8,128)(2,1)} %v_hbm.1, bf16[128,4096]{1,0:T(8,128)(2,1)} %h_hbm.1, f32[1,4096]{1,0:T(1,128)} %bitcast.1, bf16[256,128]{1,0:T(8,128)(2,1)} %constant.10.clone.fo_hbm, ...), custom_call_target="tpu_custom_call" | custom-call | flops 3221225472 | bytes 6291456 | tf_op jit(solution)/shard_map/long_conv/pallas_call | solution.py:254
  47.7 1.0 %copy.12 = bf16[128,4096]{1,0:T(8,128)(2,1)} copy(bf16[128,4096]{1,0:T(8,128)(2,1)S(1)} %long_conv.1) | data formatting | bytes 2097152

commit v6 on v5

--- a/solution.py
+++ b/solution.py
@@ -79,16 +79,9 @@
     )
     loads = [pltpu.make_async_copy(src, dst, in_sem.at[i]) for i, (src, dst) in enumerate(pairs)]
 
-    def load_parts(i):
-        for part in range(4):
-            rows = pl.ds(part * (TOK // 4), TOK // 4)
-            pltpu.make_async_copy(pairs[i][0].at[rows], pairs[i][1].at[rows], in_sem.at[i]).start()
-
     barrier = pltpu.get_barrier_semaphore()
     sweep(lambda peer, place: pl.semaphore_signal(barrier, inc=1, device_id=place, device_id_type=MESH))
-    for i in range(3):
-        load_parts(i)
-    for load in loads[3:]:
+    for load in loads:
         load.start()
 
     def lanes_of(chunk, block):
@@ -209,7 +202,7 @@
     def take(piece):
         arrived = recv.at[piece, others]
         pltpu.make_async_copy(arrived, arrived, recv_sem.at[piece]).wait()
-        lax.fori_loop(0, 8, functools.partial(widen, piece), 0)
+        lax.fori_loop(0, 8, functools.partial(widen, piece), 0, unroll=UNROLL)
 
     @pl.loop(0, CHUNKS)
     def _(chunk):
@@ -220,7 +213,7 @@
     def _(chunk):
         take(CHUNKS + chunk)
         lax.fori_loop(0, CC // BATCH, functools.partial(convolve, chunk), 0)
-        lax.fori_loop(0, 8, functools.partial(narrow, chunk), 0)
+        lax.fori_loop(0, 8, functools.partial(narrow, chunk), 0, unroll=UNROLL)
         give_back(chunk)
 
     def gate(chunk, block, carry):

time: 48.7 us -> 48.7 us (level)
  no operation moved by 1% of the time
where the time goes in v6:
time: 48.7 us; the launch traced here: 48.6 us
  Pallas kernels  47.6 us (98%)
  local copies, waits for them, and re-layouts  0.97 us (2%)
    pallas_call x1, Pallas kernels, shards(): pl.pallas_call(kernel, out_shape=pltpu.VMEM(whole, BF16), in_specs=[pl.Bl...  47.6 us

profile of v6, /device:TPU:1, one launch (start us, length us, event | category | flops | bytes accessed | tf_op | source)
XLA Modules:
  0.0 48.6 jit_solution(13865689741179223308)
XLA Ops:
  0.0 47.6 %long_conv.1 = bf16[128,4096]{1,0:T(8,128)(2,1)S(1)} custom-call(bf16[128,4096]{1,0:T(8,128)(2,1)} %q_hbm.1, bf16[128,4096]{1,0:T(8,128)(2,1)} %k_hbm.1, bf16[128,4096]{1,0:T(8,128)(2,1)} %v_hbm.1, bf16[128,4096]{1,0:T(8,128)(2,1)} %h_hbm.1, f32[1,4096]{1,0:T(1,128)} %bitcast.1, bf16[256,128]{1,0:T(8,128)(2,1)} %constant.10.clone.fo_hbm, ...), custom_call_target="tpu_custom_call" | custom-call | flops 3221225472 | bytes 6291456 | tf_op jit(solution)/shard_map/long_conv/pallas_call | solution.py:247
  47.6 1.0 %copy.12 = bf16[128,4096]{1,0:T(8,128)(2,1)} copy(bf16[128,4096]{1,0:T(8,128)(2,1)S(1)} %long_conv.1) | data formatting | bytes 2097152

commit v7 on v6

--- a/solution.py
+++ b/solution.py
@@ -15,7 +15,7 @@
 CHUNKS = 2
 CC = 16
 BATCH = 16
-UNROLL = 4
+UNROLL = 8
 BLOCKS = 16
 F32 = jnp.float32
 BF16 = jnp.bfloat16

time: 48.7 us -> 48.6 us (level)
  no operation moved by 1% of the time
where the time goes in v7:
time: 48.6 us; the launch traced here: 48.5 us
  Pallas kernels  47.5 us (98%)
  local copies, waits for them, and re-layouts  0.97 us (2%)
    pallas_call x1, Pallas kernels, shards(): pl.pallas_call(kernel, out_shape=pltpu.VMEM(whole, BF16), in_specs=[pl.Bl...  47.5 us
    unnamed x1, local copies, waits for them, and re-layouts  0.97 us

profile of v7, /device:TPU:1, one launch (start us, length us, event | category | flops | bytes accessed | tf_op | source)
XLA Modules:
  0.0 48.5 jit_solution(12036203098032471554)
XLA Ops:
  0.0 47.5 %long_conv.1 = bf16[128,4096]{1,0:T(8,128)(2,1)S(1)} custom-call(bf16[128,4096]{1,0:T(8,128)(2,1)} %q_hbm.1, bf16[128,4096]{1,0:T(8,128)(2,1)} %k_hbm.1, bf16[128,4096]{1,0:T(8,128)(2,1)} %v_hbm.1, bf16[128,4096]{1,0:T(8,128)(2,1)} %h_hbm.1, f32[1,4096]{1,0:T(1,128)} %bitcast.1, bf16[256,128]{1,0:T(8,128)(2,1)} %constant.10.clone.fo_hbm, ...), custom_call_target="tpu_custom_call" | custom-call | flops 3221225472 | bytes 6291456 | tf_op jit(solution)/shard_map/long_conv/pallas_call | solution.py:247
  47.5 1.0 %copy.12 = bf16[128,4096]{1,0:T(8,128)(2,1)} copy(bf16[128,4096]{1,0:T(8,128)(2,1)S(1)} %long_conv.1) | data formatting | bytes 2097152
